TPU v7x, 256 devices: a whole 4x4x8 slice. The times are simulated.
256 devices in a mesh: wide: 64 (over y, z_hi, x, core), narrow: 4 (over z_lo).
Axes of the slice: x: 4, y: 4, z: 8 (z_hi: 2, z_lo: 4; z = z_hi * 4 + z_lo), core: 2. Of those that a mesh axis runs over, the one named last changes fastest.
Arguments:
- frames: bfloat16 [262144, 512], P(('wide', 'narrow')), may hold values from -6 to 6
- codebook: bfloat16 [262144, 512], P(('wide', 'narrow')), may hold values from -6 to 6
- linear_map: bfloat16 [512, 512], replicated, may hold values from -0.25 to 0.25
- code_tile: int32 [262144, 1], P(('wide', 'narrow')), may hold values from 0 to 255; in each aligned block of 1024 rows (0 to 1023, 1024 to 2047, ...) at most 8 rows name the same one
- code_offset: int32 [262144], P(('wide', 'narrow')), may hold values from 0 to 1023
- reinit_source: int32 [262144], P(('wide', 'narrow')), may hold values from 0 to 4095
Outputs:
- commitment: float32 [262144], P(('wide', 'narrow'))
- nearest: float32 [262144], P(('wide', 'narrow'))
- map_gradient: float32 [512, 512], P('wide')
- new_codebook: bfloat16 [262144, 512], P(('wide', 'narrow'))
Inputs may be any that keep to these rules, and one draw needn't show every extreme that they name: `code_tile`: among the 1024 frames of one device no tile is named by more than 8 frames, a bound that some block reaches.
All inputs are finite; a program needn't handle non-finite values.
Results may differ from a plain program's by a relative error of at most 0.0024.
Values may be sent and summed in bfloat16 or wider, within the bound.
A program may use at most 64 MiB of HBM per device.

v0:
```python
import jax
import jax.numpy as jnp
from jax import lax
from jax.sharding import PartitionSpec as P


def shards(frames, codebook, linear_map, code_tile, code_offset, reinit_source):
    wide_size = lax.axis_size("wide")
    narrow_size = lax.axis_size("narrow")
    device_count = wide_size * narrow_size
    frame_rows, model_width = frames.shape
    tile_codes = codebook.shape[0]
    capacity = max(2, 2 * frame_rows // device_count)
    slot_count = device_count * capacity
    targets = code_tile.reshape(frame_rows)
    matches = targets[:, None] == targets[None, :]
    before = (
        jnp.arange(frame_rows, dtype=jnp.int32)[None, :]
        < jnp.arange(frame_rows, dtype=jnp.int32)[:, None]
    )
    ranking = jnp.sum((matches & before).astype(jnp.int32), axis=1)
    position = targets * capacity + ranking
    outgoing = jnp.zeros((slot_count, model_width), jnp.bfloat16).at[position].set(frames)
    labels = jnp.full((slot_count,), -1, jnp.int32).at[position].set(code_offset)
    arrived, arrived_labels = (
        lax.all_to_all(
            lax.all_to_all(
                outgoing.reshape(wide_size, narrow_size, capacity, model_width),
                "wide",
                split_axis=0,
                concat_axis=0,
                tiled=True,
            ),
            "narrow",
            split_axis=1,
            concat_axis=1,
            tiled=True,
        ),
        lax.all_to_all(
            lax.all_to_all(
                labels.reshape(wide_size, narrow_size, capacity),
                "wide",
                split_axis=0,
                concat_axis=0,
                tiled=True,
            ),
            "narrow",
            split_axis=1,
            concat_axis=1,
            tiled=True,
        ),
    )
    tile_effective = jnp.dot(codebook, linear_map, preferred_element_type=jnp.float32).astype(
        jnp.bfloat16
    )
    received = arrived.reshape(slot_count, model_width)
    offsets = arrived_labels.reshape(slot_count)
    selector = (offsets[:, None] == jnp.arange(tile_codes, dtype=jnp.int32)[None, :]).astype(
        jnp.bfloat16
    )
    quantized = jnp.dot(selector, tile_effective, preferred_element_type=jnp.float32)
    chosen = jnp.dot(selector, codebook, preferred_element_type=jnp.float32).astype(jnp.bfloat16)
    received_f = received.astype(jnp.float32)
    commitment = jnp.sum((received_f - quantized) ** 2, axis=1) / model_width
    effective_f = tile_effective.astype(jnp.float32)
    cross = lax.dot_general(
        received, tile_effective, (((1,), (1,)), ((), ())), preferred_element_type=jnp.float32
    )
    frame_norm = jnp.sum(received_f * received_f, axis=1)
    code_norm = jnp.sum(effective_f * effective_f, axis=1)
    nearest = jnp.min(frame_norm[:, None] - 2.0 * cross + code_norm[None, :], axis=1) / model_width
    returned = (
        lax.all_to_all(
            lax.all_to_all(
                commitment.reshape(wide_size, narrow_size, capacity),
                "wide",
                split_axis=0,
                concat_axis=0,
                tiled=True,
            ),
            "narrow",
            split_axis=1,
            concat_axis=1,
            tiled=True,
        ),
        lax.all_to_all(
            lax.all_to_all(
                nearest.reshape(wide_size, narrow_size, capacity),
                "wide",
                split_axis=0,
                concat_axis=0,
                tiled=True,
            ),
            "narrow",
            split_axis=1,
            concat_axis=1,
            tiled=True,
        ),
    )
    commitment_home = returned[0].reshape(slot_count)[position]
    nearest_home = returned[1].reshape(slot_count)[position]
    difference = (quantized - received_f).astype(jnp.bfloat16)
    scale = 2.0 / jnp.sqrt(jnp.float32(frame_rows * device_count))
    share = model_width // wide_size
    term = lax.dot_general(
        chosen, difference, (((0,), (0,)), ((), ())), preferred_element_type=jnp.float32
    )
    summed = lax.psum(term, ("wide", "narrow"))
    gradient = lax.dynamic_slice_in_dim(summed, lax.axis_index("wide") * share, share, 0)
    map_gradient = gradient * scale
    usage = jnp.sum(selector.astype(jnp.float32), axis=0)
    gathered = lax.all_gather(frames, "narrow", axis=0, tiled=True)
    fresh_rows = gathered[reinit_source]
    new_codebook = jnp.where((usage == 0.0)[:, None], fresh_rows, codebook)
    return (commitment_home, nearest_home, map_gradient, new_codebook)


def solution(mesh):
    placed = (
        P(("wide", "narrow"), None),
        P(("wide", "narrow"), None),
        P(),
        P(("wide", "narrow"), None),
        P(("wide", "narrow")),
        P(("wide", "narrow")),
    )
    return jax.shard_map(
        shards,
        mesh=mesh,
        in_specs=placed,
        out_specs=(
            P(("wide", "narrow")),
            P(("wide", "narrow")),
            P("wide", None),
            P(("wide", "narrow"), None),
        ),
        check_vma=False,
    )
```

profile of v0, /device:TPU:8, one launch (start us, length us, event | category | flops | bytes accessed | tf_op | source)
XLA Modules:
  0.0 526.0 jit_solution(11381434800669827433)
XLA Ops:
  10.0 4.5 scatter_custom_fusion.1
  15.3 14.6 %all-to-all-start.2 = ((s32[64,4,8]{2,1,0:T(4,128)}), s32[64,4,8]{2,1,0:T(4,128)S(1)}, u32[]{:S(2)}, u32[]{:S(2)}) async-start(s32[64,4,8]{2,1,0:T(4,128)} %reshape.44), calls=%async_computation.2 | async-start | bytes 262144 | tf_op jit(solution)/shard_map/all_to_all | solution.py:40
  29.9 7.2 %scatter_custom_fusion = bf16[2048,512]{1,0:T(8,128)(2,1)} fusion(s32[1024]{0:T(1024)S(1)} %bitcast.29, bf16[1024,512]{1,0:T(8,128)(2,1)} %param.6, bf16[]{:T(256)} %constant.14.clone.1), kind=kCustom, calls=%fused_computation.26 | custom fusion | bytes 2097664 | tf_op jit(solution)/shard_map/scatter | solution.py:23
  37.1 4.4 all-to-all-done.2
  41.5 8.3 %all-to-all-start = ((bf16[64,4,8,512]{3,2,1,0:T(8,128)(2,1)}), bf16[64,4,8,512]{3,2,1,0:T(8,128)(2,1)S(1)}, u32[]{:S(2)}, u32[]{:S(2)}) async-start(bf16[64,4,8,512]{3,2,1,0:T(8,128)(2,1)} %bitcast.19), calls=%async_computation | async-start | bytes 4194304 | tf_op jit(solution)/shard_map/all_to_all | solution.py:27
  51.4 46.4 %all-to-all-done = bf16[64,4,8,512]{3,2,1,0:T(8,128)(2,1)S(1)} async-done(((bf16[64,4,8,512]{3,2,1,0:T(8,128)(2,1)}), bf16[64,4,8,512]{3,2,1,0:T(8,128)(2,1)S(1)}, u32[]{:S(2)}, u32[]{:S(2)}) %all-to-all-start) | async-done | bytes 2097184 | tf_op jit(solution)/shard_map/all_to_all | solution.py:27
  97.8 42.6 %all-to-all-start.3 = ((s32[4,1,512]{2,1,0:T(1,128)}), s32[4,1,512]{2,1,0:T(1,128)S(1)}, u32[]{:S(2)}, u32[]{:S(2)}) async-start(s32[4,1,512]{2,1,0:T(1,128)} %reshape.92), calls=%async_computation.3 | async-start | bytes 16384 | tf_op jit(solution)/shard_map/all_to_all | solution.py:39
  141.9 4.1 all-to-all-done.3
  146.0 3.8 all-to-all-start.1
  155.3 54.9 %all-to-all-done.1 = bf16[64,4,8,512]{3,2,0,1:T(8,128)(2,1)S(1)} async-done(((bf16[64,4,8,512]{3,2,0,1:T(8,128)(2,1)}), bf16[64,4,8,512]{3,2,0,1:T(8,128)(2,1)S(1)}, u32[]{:S(2)}, u32[]{:S(2)}) %all-to-all-start.1) | async-done | bytes 2097184 | tf_op jit(solution)/shard_map/all_to_all | solution.py:26
  212.6 4.1 copy.32
  216.7 3.9 add_reduce_fusion
  221.5 11.8 %all-to-all-start.6 = ((f32[64,4,8]{2,1,0:T(4,128)}), f32[64,4,8]{2,1,0:T(4,128)S(1)}, u32[]{:S(2)}, u32[]{:S(2)}) async-start(f32[64,4,8]{2,1,0:T(4,128)} %div.13), calls=%async_computation.6 | async-start | bytes 262144 | tf_op jit(solution)/shard_map/all_to_all | solution.py:87
  233.3 6.0 %fusion.4 = (f32[2048]{0:T(1024)S(1)}, f32[2048,512]{0,1:T(8,128)}) fusion(bf16[2048,512]{0,1:T(8,128)(2,1)} %copy.32, bf16[1024,512]{0,1:T(8,128)(2,1)} %get-tuple-element.7, s32[2048]{0:T(1024)S(1)} %eq.44), kind=kOutput, calls=%fused_computation.14 | convolution fusion | flops 2153773056 | bytes 7356416 | tf_op jit(solution)/shard_map/dot_general | solution.py:61
  240.2 4.6 all-to-all-done.6
  244.7 8.2 %all-to-all-start.4 = ((f32[64,4,8]{2,1,0:T(4,128)}), f32[64,4,8]{2,1,0:T(4,128)S(1)}, u32[]{:S(2)}, u32[]{:S(2)}) async-start(f32[64,4,8]{2,1,0:T(4,128)} %div.11), calls=%async_computation.4 | async-start | bytes 262144 | tf_op jit(solution)/shard_map/all_to_all | solution.py:74
  253.2 7.2 %fusion.10 = f32[512,512]{1,0:T(8,128)} fusion(f32[2048,512]{0,1:T(8,128)} %get-tuple-element.5, bf16[2048,512]{0,1:T(8,128)(2,1)S(1)} %copy-done.2, bf16[1024,512]{1,0:T(8,128)(2,1)} %param.7, s32[2048]{0:T(1024)S(1)} %eq.44), kind=kOutput, calls=%fused_computation.23 | convolution fusion | flops 3227516928 | bytes 8396800 | tf_op jit(solution)/shard_map/dot_general | solution.py:105
  261.2 3.1 all-to-all-done.4
  264.4 3.2 all-to-all-start.7
  267.7 6.8 %gather_fusion.2 = bf16[1024,512]{1,0:T(8,128)(2,1)S(1)} fusion(bf16[4096,512]{1,0:T(8,128)(2,1)} %all-gather.2.cloned.1.call-done, s32[1024]{0:T(1024)S(1)} %fusion.14), kind=kCustom, calls=%fused_computation.2 | custom fusion | bytes 2101248 | tf_op jit(solution)/shard_map/gather | solution.py:113
  275.3 5.0 all-to-all-start.5
  286.9 10.5 %gather_fusion.1 = f32[1024]{0:T(1024)} fusion(f32[2048]{0:T(1024)S(1)} %reshape.46, s32[1024]{0:T(1024)S(1)} %broadcast_clamp_fusion), kind=kCustom, calls=%fused_computation.1 | custom fusion | bytes 12288 | tf_op jit(solution)/shard_map/gather | solution.py:101
  297.5 10.5 %gather_fusion = f32[1024]{0:T(1024)} fusion(f32[2048]{0:T(1024)S(1)} %reshape.45, s32[1024]{0:T(1024)S(1)} %broadcast_clamp_fusion), kind=kCustom, calls=%fused_computation | custom fusion | bytes 12288 | tf_op jit(solution)/shard_map/gather | solution.py:100
  308.0 209.2 %all-reduce.2.cloned.1.call-done = f32[512,512]{1,0:T(8,128)} async-done(((f32[512,512]{1,0:T(8,128)}), f32[512,512]{1,0:T(8,128)}) %all-reduce.2.cloned.1.call-update) | async-done | bytes 1048592 | tf_op jit(solution)/shard_map/psum | solution.py:108
  (56 shorter events, 25.2 us)
Async XLA Ops:
  8.0 141.8 %copy-start = (bf16[512,512]{1,0:T(8,128)(2,1)S(1)}, bf16[512,512]{1,0:T(8,128)(2,1)}, u32[]{:S(2)}) copy-start(bf16[512,512]{1,0:T(8,128)(2,1)} %param.8) | copy-start | bytes 1572868
  15.3 26.2 %all-to-all-start.2 = ((s32[64,4,8]{2,1,0:T(4,128)}), s32[64,4,8]{2,1,0:T(4,128)S(1)}, u32[]{:S(2)}, u32[]{:S(2)}) async-start(s32[64,4,8]{2,1,0:T(4,128)} %reshape.44), calls=%async_computation.2 | async-start | bytes 262144 | tf_op jit(solution)/shard_map/all_to_all | solution.py:40
  41.5 56.3 %all-to-all-start = ((bf16[64,4,8,512]{3,2,1,0:T(8,128)(2,1)}), bf16[64,4,8,512]{3,2,1,0:T(8,128)(2,1)S(1)}, u32[]{:S(2)}, u32[]{:S(2)}) async-start(bf16[64,4,8,512]{3,2,1,0:T(8,128)(2,1)} %bitcast.19), calls=%async_computation | async-start | bytes 4194304 | tf_op jit(solution)/shard_map/all_to_all | solution.py:27
  49.8 217.8 %all-gather.2.cloned.1.call-start = ((), (), s32[]{:S(2)}) async-start(), calls=%async_computation.9 | async-start | bytes 5242880 | tf_op jit(solution)/shard_map/all_gather | solution.py:112
  97.8 48.2 %all-to-all-start.3 = ((s32[4,1,512]{2,1,0:T(1,128)}), s32[4,1,512]{2,1,0:T(1,128)S(1)}, u32[]{:S(2)}, u32[]{:S(2)}) async-start(s32[4,1,512]{2,1,0:T(1,128)} %reshape.92), calls=%async_computation.3 | async-start | bytes 16384 | tf_op jit(solution)/shard_map/all_to_all | solution.py:39
  140.4 9.4 %copy-start.4 = (s32[1024]{0:T(1024)S(1)}, s32[1024]{0:T(1024)}, u32[]{:S(2)}) copy-start(s32[1024]{0:T(1024)} %param.11) | copy-start | bytes 12292
  146.0 64.3 %all-to-all-start.1 = ((bf16[64,4,8,512]{3,2,0,1:T(8,128)(2,1)}), bf16[64,4,8,512]{3,2,0,1:T(8,128)(2,1)S(1)}, u32[]{:S(2)}, u32[]{:S(2)}) async-start(bf16[64,4,8,512]{3,2,0,1:T(8,128)(2,1)} %copy.30), calls=%async_computation.1 | async-start | bytes 4194304 | tf_op jit(solution)/shard_map/all_to_all | solution.py:26
  212.6 4.1 copy-start.1
  221.5 23.2 %all-to-all-start.6 = ((f32[64,4,8]{2,1,0:T(4,128)}), f32[64,4,8]{2,1,0:T(4,128)S(1)}, u32[]{:S(2)}, u32[]{:S(2)}) async-start(f32[64,4,8]{2,1,0:T(4,128)} %div.13), calls=%async_computation.6 | async-start | bytes 262144 | tf_op jit(solution)/shard_map/all_to_all | solution.py:87
  233.3 19.9 %copy-start.2 = (bf16[2048,512]{0,1:T(8,128)(2,1)S(1)}, bf16[2048,512]{0,1:T(8,128)(2,1)}, u32[]{:S(2)}) copy-start(bf16[2048,512]{0,1:T(8,128)(2,1)} %copy.32) | copy-start | bytes 6291460
  244.7 19.6 %all-to-all-start.4 = ((f32[64,4,8]{2,1,0:T(4,128)}), f32[64,4,8]{2,1,0:T(4,128)S(1)}, u32[]{:S(2)}, u32[]{:S(2)}) async-start(f32[64,4,8]{2,1,0:T(4,128)} %div.11), calls=%async_computation.4 | async-start | bytes 262144 | tf_op jit(solution)/shard_map/all_to_all | solution.py:74
  252.9 264.3 %all-reduce.2.cloned.1.call-start = ((), (), s32[]{:S(2)}) async-start(), calls=%async_computation.8 | async-start | bytes 2097152 | tf_op jit(solution)/shard_map/psum | solution.py:108
  264.4 10.9 %all-to-all-start.7 = ((f32[4,1,512]{2,1,0:T(1,128)}), f32[4,1,512]{2,1,0:T(1,128)S(1)}, u32[]{:S(2)}, u32[]{:S(2)}) async-start(f32[4,1,512]{2,1,0:T(1,128)} %reshape.96), calls=%async_computation.7 | async-start | bytes 16384 | tf_op jit(solution)/shard_map/all_to_all | solution.py:86
  267.6 12.7 %copy-start.3 = (bf16[1024,512]{1,0:T(8,128)(2,1)S(1)}, bf16[1024,512]{1,0:T(8,128)(2,1)}, u32[]{:S(2)}) copy-start(bf16[1024,512]{1,0:T(8,128)(2,1)} %param.7) | copy-start | bytes 3145732
  275.3 10.6 %all-to-all-start.5 = ((f32[4,1,512]{2,1,0:T(1,128)}), f32[4,1,512]{2,1,0:T(1,128)S(1)}, u32[]{:S(2)}, u32[]{:S(2)}) async-start(f32[4,1,512]{2,1,0:T(1,128)} %reshape.94), calls=%async_computation.5 | async-start | bytes 16384 | tf_op jit(solution)/shard_map/all_to_all | solution.py:73
Sparse Core Ops, SparseCore 0:
  52.6 128.0 all-gather.1
Sparse Core Ops, SparseCore 1:
  260.6 256.6 all-reduce.1
where the time goes:
time: 527 us; the launch traced here: 526 us
  waiting for transfers between devices  330 us (63%)
  starting transfers between devices  97.8 us (19%)
  local copies, waits for them, and re-layouts  54 us (10%)
  matrix products  20.1 us (4%)
  between operations  15.7 us (3%)
  other arithmetic  7.98 us (2%)
    psum x1, waiting for transfers between devices, shards(): summed = lax.psum(term, ('wide', 'narrow'))  209 us
    all_to_all x1, waiting for transfers between devices, shards(): lax.all_to_all(lax.all_to_all(outgoing.reshape(wide_size, narrow_size, ca...  54.9 us
    all_to_all x1, waiting for transfers between devices, shards(): lax.all_to_all(outgoing.reshape(wide_size, narrow_size, capacity, model_w...  46.4 us
    all_to_all x1, starting transfers between devices, shards(): lax.all_to_all(lax.all_to_all(labels.reshape(wide_size, narrow_size, capa...  42.6 us
    all_to_all x1, starting transfers between devices, shards(): lax.all_to_all(labels.reshape(wide_size, narrow_size, capacity), 'wide',...  14.6 us
    all_to_all x1, starting transfers between devices, shards(): lax.all_to_all(nearest.reshape(wide_size, narrow_size, capacity), 'wide',...  11.8 us
    gather x1, local copies, waits for them, and re-layouts, shards(): nearest_home = returned[1].reshape(slot_count)[position]  10.5 us
  transfers between devices with their start and end apart: 10, of which 8 were waited for; matrix products, arithmetic and copies ran while one was open for 14% of the time, Pallas kernels for 0%

commit v1 on v0

v1 whole, which is shorter than its diff:
```python
import functools

import jax
import jax.numpy as jnp
from jax import lax
from jax.experimental import pallas as pl
from jax.experimental.pallas import tpu as pltpu
from jax.sharding import PartitionSpec as P

MESH = pl.DeviceIdType.MESH
F32 = jnp.float32
BF16 = jnp.bfloat16

ROWS = 1024
WIDTH = 512
DEVICES = 256
CAP = 8
GROUPS = 8
PER_GROUP = DEVICES // GROUPS
SLOTS = PER_GROUP * CAP
HALF = WIDTH // 2
BLOCK = 2 * CAP
FETCH = 320
SEND_AT = 2


def coordinates():
    wide = lax.axis_index("wide")
    narrow = lax.axis_index("narrow")
    return (wide // 2) % 4, wide // 16, ((wide // 8) % 2) * 4 + narrow, wide % 2


def device(x, y, z, core):
    return {"wide": ((y * 2 + z // 4) * 4 + x) * 2 + core, "narrow": lax.rem(z, 4)}


def ahead(step, here):
    x, y, z, core = here
    return device(
        lax.rem(x + (step // 16) % 4, 4),
        lax.rem(y + step // 64, 4),
        lax.rem(z + step % 8, 8),
        lax.rem(core + (step // 8) % 2, 2),
    )


def behind(step, here):
    x, y, z, core = here
    return device(
        lax.rem(x + 4 - (step // 16) % 4, 4),
        lax.rem(y + 4 - step // 64, 4),
        lax.rem(z + 8 - step % 8, 8),
        lax.rem(core + (step // 8) % 2, 2),
    )


def iota(shape, dim):
    return lax.broadcasted_iota(jnp.int32, shape, dim)


def nn(a, b):
    return lax.dot_general(a, b, (((1,), (0,)), ((), ())), preferred_element_type=F32)


def nt(a, b):
    return lax.dot_general(a, b, (((1,), (1,)), ((), ())), preferred_element_type=F32)


def tn(a, b):
    return lax.dot_general(a, b, (((0,), (0,)), ((), ())), preferred_element_type=F32)


def one(mask):
    return jnp.where(mask, 1.0, 0.0).astype(BF16)


def remote(src, dst, send, recv, target):
    return pltpu.make_async_remote_copy(
        src_ref=src, dst_ref=dst, send_sem=send, recv_sem=recv, device_id=target, device_id_type=MESH
    )


def drain(ref, sem):
    pltpu.make_async_copy(ref, ref, sem).wait()


def fetch_ranks(source, before):
    owner = source >> 10
    owners = one(owner == iota((16, ROWS), 0))
    counts = nn(owners, before)
    return jnp.sum(owners.astype(F32) * counts, axis=0, keepdims=True).astype(jnp.int32)


def step_kernel(
    frames, codebook, linear_map, tile, offset, source,
    commit_out, near_out, grad_out, fresh_out, used_out, over_out,
    outgoing, arrived, labels_out, labels_in, results_out, results_in,
    before, effective, code_norm, place, usage, total,
    half_in, half_sum, plane_in, plane_sum, column_in,
    asked, rows_out, rows_in, fresh,
    data_send, data_recv, label_send, label_recv, result_send, result_recv,
    half_send, half_recv, plane_send, plane_recv, column_send, column_recv,
    ask_send, ask_recv, row_send, row_recv, ready,
):
    here = coordinates()
    x, y, z, core = here
    narrow = lax.axis_index("narrow")

    barrier = pltpu.get_barrier_semaphore()

    def greet(sem, first, last, stride):
        def body(step, carry):
            pl.semaphore_signal(sem, inc=1, device_id=ahead(step * stride, here), device_id_type=MESH)
            return carry

        lax.fori_loop(first, last, body, 0)

    greet(barrier, 1, 8, 1)
    greet(barrier, 1, 32, 8)

    before[...] = one(iota((ROWS, ROWS), 0) < iota((ROWS, ROWS), 1))
    named = tile[...]
    wide = named >> 2
    depth = ((wide >> 3) & 1) * 4 + (named & 3)
    step_of = (
        ((depth + 8 - z) & 7)
        + 8 * (((wide & 1) + 2 - core) & 1)
        + 16 * ((((wide >> 1) & 3) + 4 - x) & 3)
        + 64 * (((wide >> 4) + 4 - y) & 3)
    )
    chosen_step = one(step_of == iota((DEVICES, ROWS), 0))
    earlier = nn(chosen_step, before[...])
    rank = jnp.sum(chosen_step.astype(F32) * earlier, axis=0, keepdims=True).astype(jnp.int32)
    place[0:1, :] = step_of
    place[1:2, :] = rank
    place[2:3, :] = step_of * CAP + rank
    fetch_rank = fetch_ranks(source[...], before[...])
    place[3:4, :] = fetch_rank
    far = (source[...] >> 10) != narrow
    over = jnp.max(jnp.where(far & (fetch_rank >= FETCH), 1.0, 0.0), axis=1, keepdims=True)

    label = offset[...] + 1
    at_rank = rank == iota((128, ROWS), 0)
    high = jnp.where(at_rank, (label >> 5).astype(F32), 0.0).astype(BF16)
    low = jnp.where(at_rank, (label & 31).astype(F32), 0.0).astype(BF16)
    marks = 32.0 * nt(chosen_step, high) + nt(chosen_step, low)
    marks = jnp.where(iota((DEVICES, 128), 1) == 127, over, marks)
    labels_out[...] = marks.reshape(DEVICES, 1, 128)

    def dispatch(group, carry):
        slots = iota((SLOTS, ROWS), 0) + group * SLOTS
        picked = nn(one(place[2:3, :] == slots), frames[...])
        left = picked[:, :HALF].reshape(PER_GROUP, 1, CAP, HALF)
        right = picked[:, HALF:].reshape(PER_GROUP, 1, CAP, HALF)
        block = jnp.concatenate([left, right], axis=1).reshape(2 * SLOTS, HALF)
        outgoing[pl.ds(pl.multiple_of(group * 2 * SLOTS, 2 * SLOTS), 2 * SLOTS), :] = block.astype(BF16)
        return carry

    lax.fori_loop(0, GROUPS, dispatch, 0)

    pl.semaphore_wait(barrier, 38)
    greet(ready, 1, 8, 1)
    pl.semaphore_wait(ready, 7)

    for j in range(3):
        target = {"narrow": lax.rem(narrow + j + 1, 4)}
        remote(source, asked.at[j], ask_send, ask_recv.at[j], target).start()

    own_data = pltpu.make_async_copy(outgoing.at[pl.ds(0, BLOCK)], arrived.at[pl.ds(0, BLOCK)], data_recv.at[0])
    own_data.start()
    own_label = pltpu.make_async_copy(labels_out.at[0], labels_in.at[0], label_recv.at[0])
    own_label.start()

    def send(step, carry):
        target = ahead(step, here)
        group = step // PER_GROUP
        rows = pl.ds(pl.multiple_of(step * BLOCK, BLOCK), BLOCK)
        remote(labels_out.at[step], labels_in.at[step], label_send, label_recv.at[group], target).start()
        remote(outgoing.at[rows], arrived.at[rows], data_send, data_recv.at[group], target).start()
        return carry

    lax.fori_loop(1, DEVICES, send, 0)

    eff = nn(codebook[...], linear_map[...]).astype(BF16)
    effective[...] = eff
    eff_f = eff.astype(F32)
    norms = jnp.sum(eff_f * eff_f, axis=1, keepdims=True)
    code_norm[...] = jnp.transpose(jnp.broadcast_to(norms, (ROWS, 128)))[0:1, :]
    usage[...] = jnp.zeros_like(usage)
    total[...] = jnp.zeros_like(total)

    for j in range(3):
        drain(asked.at[j], ask_recv.at[j])
        wanted = asked[j]
        order = fetch_ranks(wanted, before[...])
        mine = ((wanted >> 10) == narrow) & (order == iota((FETCH, ROWS), 0))
        index = jnp.sum(jnp.where(mine, (wanted & 1023).astype(F32), 0.0), axis=1, keepdims=True)
        rows = one(index.astype(jnp.int32) == iota((FETCH, ROWS), 1))
        rows_out[j] = nn(rows, frames[...]).astype(BF16)

    def work(group, carry):
        rows = pl.ds(pl.multiple_of(group * 2 * SLOTS, 2 * SLOTS), 2 * SLOTS)
        messages = pl.ds(group * PER_GROUP, PER_GROUP)
        drain(labels_in.at[messages], label_recv.at[group])
        drain(arrived.at[rows], data_recv.at[group])

        @pl.when(group == SEND_AT)
        def _():
            for j in range(3):
                target = {"narrow": lax.rem(narrow + 3 - j, 4)}
                remote(rows_out.at[j], rows_in.at[j], row_send, row_recv.at[j], target).start()

        parts = arrived[rows, :].astype(F32).reshape(PER_GROUP, 2, CAP, HALF)
        taken_f = jnp.concatenate(
            [parts[:, 0].reshape(SLOTS, HALF), parts[:, 1].reshape(SLOTS, HALF)], axis=1
        )
        taken = taken_f.astype(BF16)
        spread = jnp.broadcast_to(labels_in[messages], (PER_GROUP, CAP, 128)).reshape(SLOTS, 128)
        row_rank = iota((SLOTS, 128), 0) & (CAP - 1)
        lane = iota((SLOTS, 128), 1)
        mark = jnp.sum(jnp.where(lane == row_rank, spread, 0.0), axis=1, keepdims=True)
        code = mark.astype(jnp.int32) - 1
        chosen_mask = code == iota((SLOTS, ROWS), 1)
        selector = one(chosen_mask)
        usage[...] += jnp.sum(jnp.where(chosen_mask, 1.0, 0.0), axis=0, keepdims=True)
        quantized = nn(selector, effective[...])
        chosen = nn(selector, codebook[...]).astype(BF16)
        gap = quantized - taken_f
        commitment = jnp.sum(gap * gap, axis=1, keepdims=True) * (1.0 / WIDTH)
        cross = nt(taken, effective[...])
        least = jnp.min(code_norm[...] - 2.0 * cross, axis=1, keepdims=True)
        nearest = (jnp.sum(taken_f * taken_f, axis=1, keepdims=True) + least) * (1.0 / WIDTH)
        total[...] += tn(chosen, gap.astype(BF16)).reshape(total.shape)
        back = jnp.where(lane == row_rank, commitment, 0.0) + jnp.where(lane == row_rank + CAP, nearest, 0.0)
        results_out[messages] = jnp.sum(back.reshape(PER_GROUP, CAP, 128), axis=1, keepdims=True)

        def give(step, carry):
            @pl.when(step > 0)
            def _():
                remote(
                    results_out.at[step], results_in.at[step], result_send, result_recv, behind(step, here)
                ).start()

            @pl.when(step == 0)
            def _():
                pltpu.make_async_copy(results_out.at[0], results_in.at[0], result_recv).start()

            return carry

        lax.fori_loop(group * PER_GROUP, (group + 1) * PER_GROUP, give, 0)
        return carry

    lax.fori_loop(0, GROUPS, work, 0)

    to_pair = remote(total.at[:, :, :, 1 - core], half_in, half_send, half_recv, device(x, y, z, 1 - core))
    to_pair.start()

    wanted = source[...]
    mine = ((wanted >> 10) == narrow) & ((wanted & 1023) == iota((ROWS, ROWS), 0))
    fresh[...] = tn(one(mine), frames[...])

    to_pair.wait()
    half_sum[...] = total[:, :, :, core] + half_in[...]
    for step in range(1, 16):
        x2 = lax.rem(x + step % 4, 4)
        y2 = lax.rem(y + step // 4, 4)
        remote(
            half_sum.at[y2, :, x2], plane_in.at[step - 1], plane_send, plane_recv, device(x2, y2, z, core)
        ).start()

    drain(results_in, result_recv)
    returned = results_in[...].reshape(DEVICES, 128)
    steps = one(place[0:1, :] == iota((DEVICES, ROWS), 0))
    first = returned.astype(BF16)
    rest = returned - first.astype(F32)
    second = rest.astype(BF16)
    third = (rest - second.astype(F32)).astype(BF16)
    home = tn(first, steps) + tn(second, steps) + tn(third, steps)
    here_rank = place[1:2, :] == iota((CAP, ROWS), 0)
    commit_out[...] = jnp.sum(jnp.where(here_rank, home[0:CAP], 0.0), axis=0, keepdims=True)
    near_out[...] = jnp.sum(jnp.where(here_rank, home[CAP : 2 * CAP], 0.0), axis=0, keepdims=True)

    drain(plane_in, plane_recv)
    plane_sum[...] = half_sum[y, :, x] + jnp.sum(plane_in[...], axis=0)
    for step in range(1, 8):
        z2 = lax.rem(z + step, 8)
        remote(
            plane_sum.at[z2 // 4], column_in.at[step - 1], column_send, column_recv, device(x, y, z2, core)
        ).start()

    for j in range(3):
        drain(rows_in.at[j], row_recv.at[j])
        peer = lax.rem(narrow + j + 1, 4)
        wanted = source[...]
        asked_for = ((wanted >> 10) == peer) & (place[3:4, :] == iota((FETCH, ROWS), 0))
        fresh[...] += tn(one(asked_for), rows_in[j])

    used = usage[...]
    used_out[...] = used
    used_column = jnp.transpose(jnp.broadcast_to(used, (128, ROWS)))[:, 0:1]
    fresh_out[...] = jnp.where(used_column > 0.0, codebook[...].astype(F32), fresh[...]).astype(BF16)
    over_out[...] = jnp.max(labels_in[...], axis=0)

    drain(column_in, column_recv)
    grad_out[...] = (plane_sum[z // 4] + jnp.sum(column_in[...], axis=0)) * (2.0 / 512.0)

    sent = pl.ds(BLOCK, (DEVICES - 1) * BLOCK)
    messages = pl.ds(1, DEVICES - 1)
    drain(outgoing.at[sent], data_send)
    drain(labels_out.at[messages], label_send)
    drain(results_out.at[messages], result_send)
    drain(plane_in, plane_send)
    drain(column_in, column_send)
    drain(asked, ask_send)
    drain(rows_out, row_send)


def exchange(frames, codebook, linear_map, tile, offset, source):
    vmem = pl.BlockSpec(memory_space=pltpu.VMEM)
    dma = pltpu.SemaphoreType.DMA
    return pl.pallas_call(
        step_kernel,
        out_shape=[
            jax.ShapeDtypeStruct((1, ROWS), F32),
            jax.ShapeDtypeStruct((1, ROWS), F32),
            jax.ShapeDtypeStruct((CAP, WIDTH), F32),
            jax.ShapeDtypeStruct((ROWS, WIDTH), BF16),
            jax.ShapeDtypeStruct((1, ROWS), F32),
            jax.ShapeDtypeStruct((1, 128), F32),
        ],
        in_specs=[vmem] * 6,
        out_specs=[vmem] * 6,
        scratch_shapes=[
            pltpu.VMEM((DEVICES * BLOCK, HALF), BF16),
            pltpu.VMEM((DEVICES * BLOCK, HALF), BF16),
            pltpu.VMEM((DEVICES, 1, 128), F32),
            pltpu.VMEM((DEVICES, 1, 128), F32),
            pltpu.VMEM((DEVICES, 1, 128), F32),
            pltpu.VMEM((DEVICES, 1, 128), F32),
            pltpu.VMEM((ROWS, ROWS), BF16),
            pltpu.VMEM((ROWS, WIDTH), BF16),
            pltpu.VMEM((1, ROWS), F32),
            pltpu.VMEM((8, ROWS), jnp.int32),
            pltpu.VMEM((1, ROWS), F32),
            pltpu.VMEM((4, 2, 4, 2, 8, WIDTH), F32),
            pltpu.VMEM((4, 2, 4, 8, WIDTH), F32),
            pltpu.VMEM((4, 2, 4, 8, WIDTH), F32),
            pltpu.VMEM((15, 2, 8, WIDTH), F32),
            pltpu.VMEM((2, 8, WIDTH), F32),
            pltpu.VMEM((7, 8, WIDTH), F32),
            pltpu.VMEM((3, 1, ROWS), jnp.int32),
            pltpu.VMEM((3, FETCH, WIDTH), BF16),
            pltpu.VMEM((3, FETCH, WIDTH), BF16),
            pltpu.VMEM((ROWS, WIDTH), F32),
            dma, dma((GROUPS,)), dma, dma((GROUPS,)), dma, dma,
            dma, dma, dma, dma, dma, dma,
            dma, dma((3,)), dma, dma((3,)), pltpu.SemaphoreType.REGULAR,
        ],
        compiler_params=pltpu.CompilerParams(
            collective_id=0, has_side_effects=True, vmem_limit_bytes=52 * 2**20
        ),
    )(frames, codebook, linear_map, tile, offset, source)


def shards(frames, codebook, linear_map, code_tile, code_offset, reinit_source):
    commitment, nearest, gradient, fresh, used, over = exchange(
        frames,
        codebook,
        linear_map,
        code_tile.reshape(1, ROWS),
        code_offset.reshape(1, ROWS),
        reinit_source.reshape(1, ROWS),
    )

    def whole_gather():
        group = lax.all_gather(frames, "narrow", axis=0, tiled=True)
        return jnp.where(used.reshape(ROWS, 1) > 0.0, codebook, group[reinit_source])

    new_codebook = lax.cond(over[0, 127] > 0.0, whole_gather, lambda: fresh)
    return commitment.reshape(ROWS), nearest.reshape(ROWS), gradient, new_codebook


def solution(mesh):
    placed = (
        P(("wide", "narrow"), None),
        P(("wide", "narrow"), None),
        P(),
        P(("wide", "narrow"), None),
        P(("wide", "narrow")),
        P(("wide", "narrow")),
    )
    return jax.shard_map(
        shards,
        mesh=mesh,
        in_specs=placed,
        out_specs=(
            P(("wide", "narrow")),
            P(("wide", "narrow")),
            P("wide", None),
            P(("wide", "narrow"), None),
        ),
        check_vma=False,
    )
```

time: 527 us -> 131 us (0.25)
  waiting for transfers between devices: 330 us -> 0 us
  Pallas kernels: 0 us -> 109 us
  starting transfers between devices: 97.8 us -> 0 us
  local copies, waits for them, and re-layouts: 54 us -> 5.75 us
  matrix products: 20.1 us -> 0 us
  other arithmetic: 7.98 us -> 0 us
    psum x1 -> x0, waiting for transfers between devices: 209 us -> none  [shards(): summed = lax.psum(term, ('wide', 'narrow'))]
    all_to_all x8 -> x0, waiting for transfers between devices: 120 us -> none  [the longest x1 54.9 us: shards(): lax.all_to_all(lax.all_to_all(outgoing.reshape(wide_size, narrow_size, ca...]
    pallas_call x0 -> x1, Pallas kernels: none -> 109 us  [exchange(): pl.pallas_call(step_kernel, out_shape=[jax.ShapeDtypeStruct((1, ROWS), F3...]
    all_to_all x8 -> x0, starting transfers between devices: 97.5 us -> none  [the longest x1 42.6 us: shards(): lax.all_to_all(lax.all_to_all(labels.reshape(wide_size, narrow_size, capa...]
    gather x3 -> x0, local copies, waits for them, and re-layouts: 27.9 us -> none  [the longest x1 10.5 us: shards(): nearest_home = returned[1].reshape(slot_count)[position]]
    dot_general x4 -> x0, matrix products: 20.1 us -> none  [the longest x1 7.23 us: shards(): lax.dot_general(chosen, difference, (((0,), (0,)), ((), ())), preferred_e...]
    scatter x2 -> x0, local copies, waits for them, and re-layouts: 11.6 us -> none  [the longest x1 7.17 us: shards(): jnp.zeros((slot_count, model_width), jnp.bfloat16).at[position].set(frames)]
    reshape x4 -> x0, local copies, waits for them, and re-layouts: 5.28 us -> none  [the longest x1 4.12 us: shards(): received = arrived.reshape(slot_count, model_width)]
  transfers between devices with their start and end apart: 10 -> 0, of which waited for: 8 -> 0; matrix products, arithmetic and copies ran while one was open for 14% -> 0% of each run, Pallas kernels for 0% -> 0%
where the time goes in v1:
time: 131 us; the launch traced here: 129 us
  Pallas kernels  109 us (83%)
  between operations  14.7 us (11%)
  local copies, waits for them, and re-layouts  5.75 us (4%)
    pallas_call x1, Pallas kernels, exchange(): pl.pallas_call(step_kernel, out_shape=[jax.ShapeDtypeStruct((1, ROWS), F3...  109 us
    unnamed x10, local copies, waits for them, and re-layouts  5.17 us

profile of v1, /device:TPU:8, one launch (start us, length us, event | category | flops | bytes accessed | tf_op | source)
XLA Modules:
  0.0 129.0 jit_solution(994637638117416828)
XLA Ops:
  7.2 0.0 copy-start
  7.2 1.0 copy-done
  8.2 0.0 copy-start.1
  8.2 0.7 copy-done.1
  8.9 0.0 copy-start.2
  8.9 0.7 copy-done.2
  9.6 108.6 %shard_map.93 = (f32[1,1024]{1,0:T(1,128)S(1)}, f32[1,1024]{1,0:T(1,128)S(1)}, f32[8,512]{1,0:T(8,128)S(1)}, bf16[1024,512]{1,0:T(8,128)(2,1)S(1)}, f32[1,1024]{1,0:T(1,128)S(1)}, /*index=5*/f32[1,128]{1,0:T(1,128)S(1)}) custom-call(bf16[1024,512]{1,0:T(8,128)(2,1)} %frames.1, bf16[1024,512]{1,0:T(8,128)(2,1)} %codebook.1, bf16[512,512]{1,0:T(8,128)(2,1)S(1)} %copy-done, ...), custom_call_target="tpu_custom_call" | custom-call | tf_op jit(solution)/shard_map/pallas_call | solution.py:321
  118.2 0.6 slice.3
  119.4 0.6 copy.16
  120.0 0.6 copy.17
  120.6 0.6 copy.18
  121.2 1.0 copy.19
  (1 shorter events, 0.0 us)
Async XLA Ops:
  7.2 1.0 copy-start
  8.2 0.7 copy-start.1
  8.9 0.7 copy-start.2

commit v2 on v1

v2 whole, which is shorter than its diff:
```python
import functools

import jax
import jax.numpy as jnp
from jax import lax
from jax.experimental import pallas as pl
from jax.experimental.pallas import tpu as pltpu
from jax.sharding import PartitionSpec as P

MESH = pl.DeviceIdType.MESH
F32 = jnp.float32
BF16 = jnp.bfloat16

ROWS = 1024
WIDTH = 512
DEVICES = 256
CAP = 8
GROUPS = 8
PER_GROUP = DEVICES // GROUPS
SLOTS = PER_GROUP * CAP
HALF = WIDTH // 2
BLOCK = 2 * CAP
FETCH = 208
SEND_AT = 7
PLANE = 32
DEPTH = 8
PLANE_GROUP = PLANE // GROUPS
FETCHED = 640


def coordinates():
    wide = lax.axis_index("wide")
    narrow = lax.axis_index("narrow")
    return (wide // 2) % 4, wide // 16, ((wide // 8) % 2) * 4 + narrow, wide % 2


def device(x, y, z, core):
    return {"wide": ((y * 2 + z // 4) * 4 + x) * 2 + core, "narrow": lax.rem(z, 4)}


def plane_index(step, here, sign):
    x, y, _, core = here
    x2 = lax.rem(x + 4 + sign * lax.rem(step // 2, 4), 4)
    y2 = lax.rem(y + 4 + sign * (step // 8), 4)
    return y2 * 16 + x2 * 2 + lax.rem(core + lax.rem(step, 2), 2)


def column_index(step, here, sign):
    z2 = lax.rem(here[2] + 8 + sign * step, 8)
    return (z2 // 4) * 8, lax.rem(z2, 4)


def iota(shape, dim):
    return lax.broadcasted_iota(jnp.int32, shape, dim)


def nn(a, b):
    return lax.dot_general(a, b, (((1,), (0,)), ((), ())), preferred_element_type=F32)


def nt(a, b):
    return lax.dot_general(a, b, (((1,), (1,)), ((), ())), preferred_element_type=F32)


def tn(a, b):
    return lax.dot_general(a, b, (((0,), (0,)), ((), ())), preferred_element_type=F32)


def one(mask):
    return jnp.where(mask, 1.0, 0.0).astype(BF16)


def remote(src, dst, send, recv, target):
    return pltpu.make_async_remote_copy(
        src_ref=src, dst_ref=dst, send_sem=send, recv_sem=recv, device_id=target, device_id_type=MESH
    )


def drain(ref, sem):
    pltpu.make_async_copy(ref, ref, sem).wait()


def fetch_ranks(source, before):
    owner = source >> 10
    owners = one(owner == iota((16, ROWS), 0))
    counts = nn(owners, before)
    return jnp.sum(owners.astype(F32) * counts, axis=0, keepdims=True).astype(jnp.int32)


def step_kernel(
    frames_in, codebook_in, linear_in, tile_in, offset_in, source_in,
    commit_out, near_out, grad_out, fresh_out, used_out, over_out,
    frames, codebook, linear_map, tile, offset, source, wanted_here,
    outgoing, arrived, labels_out, labels_mid, labels_in, results_out, results_mid, results_pack, results_in,
    before, effective, code_norm, place, total,
    half_in, half_sum, plane_in, plane_sum, column_in,
    asked, rows_out, rows_in, picks, fresh,
    load, data_send, data_recv, column_label_send, column_label_recv, plane_label_send, plane_label_recv,
    plane_result_send, plane_result_recv, column_result_send, column_result_recv,
    half_send, half_recv, plane_send, plane_recv, column_send, column_recv,
    ask_send, ask_recv, row_send, row_recv,
):
    here = coordinates()
    x, y, z, core = here
    narrow = lax.axis_index("narrow")

    loads = [
        pltpu.make_async_copy(src, dst, load.at[i])
        for i, (src, dst) in enumerate(
            (
                (tile_in, tile),
                (offset_in, offset),
                (source_in, source),
                (frames_in, frames),
                (codebook_in, codebook),
                (linear_in, linear_map),
            )
        )
    ]
    for copy in loads:
        copy.start()

    columns = [column_index(step, here, 1) for step in range(DEPTH)]
    plane_here = plane_index(0, here, 1)

    def target(base, step):
        return {"wide": base + columns[step][0], "narrow": columns[step][1]}

    barrier = pltpu.get_barrier_semaphore()
    for step in range(1, DEPTH):
        pl.semaphore_signal(barrier, inc=1, device_id=target(plane_here, step), device_id_type=MESH)

    def greet(step, carry):
        pl.semaphore_signal(
            barrier, inc=1, device_id=target(plane_index(step, here, 1), 0), device_id_type=MESH
        )
        return carry

    lax.fori_loop(1, PLANE, greet, 0)

    before[...] = one(iota((ROWS, ROWS), 0) < iota((ROWS, ROWS), 1))
    for copy in loads[:3]:
        copy.wait()
    named = tile[...]
    wide = named >> 2
    depth = ((wide >> 3) & 1) * 4 + (named & 3)
    step_of = (
        ((depth + 8 - z) & 7)
        + 8 * (((wide & 1) + 2 - core) & 1)
        + 16 * ((((wide >> 1) & 3) + 4 - x) & 3)
        + 64 * (((wide >> 4) + 4 - y) & 3)
    )
    chosen_step = one(step_of == iota((DEVICES, ROWS), 0))
    earlier = nn(chosen_step, before[...])
    rank = jnp.sum(chosen_step.astype(F32) * earlier, axis=0, keepdims=True).astype(jnp.int32)
    place[0:1, :] = step_of
    place[1:2, :] = rank
    place[2:3, :] = step_of * CAP + rank

    label = offset[...] + 1
    at_lane = (step_of >> 3) * CAP + rank == iota((PLANE * CAP, ROWS), 0)
    high = jnp.where(at_lane, (label >> 5).astype(F32), 0.0).astype(BF16)
    low = jnp.where(at_lane, (label & 31).astype(F32), 0.0).astype(BF16)
    chosen_depth = one((step_of & 7) == iota((16, ROWS), 0))
    marks = (32.0 * nt(chosen_depth, high) + nt(chosen_depth, low))[:DEPTH]
    labels_out[:, 0] = marks[:, :128].reshape(DEPTH, 1, 128)
    labels_out[:, 1] = marks[:, 128:].reshape(DEPTH, 1, 128)
    labels_mid[0] = labels_out[0]
    loads[3].wait()

    def dispatch(group):
        slots = iota((SLOTS, ROWS), 0) + group * SLOTS
        picked = nn(one(place[2:3, :] == slots), frames[...])
        left = picked[:, :HALF].reshape(PER_GROUP, 1, CAP, HALF)
        right = picked[:, HALF:].reshape(PER_GROUP, 1, CAP, HALF)
        block = jnp.concatenate([left, right], axis=1).reshape(2 * SLOTS, HALF)
        outgoing[pl.ds(pl.multiple_of(group * 2 * SLOTS, 2 * SLOTS), 2 * SLOTS), :] = block.astype(BF16)

    dispatch(0)

    pl.semaphore_wait(barrier, DEPTH + PLANE - 2)

    for step in range(1, DEPTH):
        remote(
            labels_out.at[step], labels_mid.at[step], column_label_send, column_label_recv,
            target(plane_here, step),
        ).start()
    drain(labels_mid.at[pl.ds(1, DEPTH - 1)], column_label_recv)

    own_label = pltpu.make_async_copy(labels_mid.at[:, 0], labels_in.at[0], plane_label_recv)
    own_label.start()

    def label_plane(step, carry):
        remote(
            labels_mid.at[:, step // 16], labels_in.at[step], plane_label_send, plane_label_recv,
            target(plane_index(step, here, 1), 0),
        ).start()
        return carry

    lax.fori_loop(1, PLANE, label_plane, 0)

    own_data = pltpu.make_async_copy(outgoing.at[pl.ds(0, BLOCK)], arrived.at[pl.ds(0, BLOCK)], data_recv.at[0])
    own_data.start()

    def send(step, first):
        base = plane_index(step, here, 1)
        start = pl.multiple_of(step * (DEPTH * BLOCK), DEPTH * BLOCK)
        for d in range(first, DEPTH):
            rows = pl.ds(start + d * BLOCK, BLOCK)
            remote(
                outgoing.at[rows], arrived.at[rows], data_send, data_recv.at[step // PLANE_GROUP], target(base, d)
            ).start()

    def send_plane(step, carry):
        send(step, 0)
        return carry

    send(0, 1)
    lax.fori_loop(1, PLANE_GROUP, send_plane, 0)

    def dispatch_and_send(group, carry):
        dispatch(group)
        lax.fori_loop(group * PLANE_GROUP, (group + 1) * PLANE_GROUP, send_plane, 0)
        return carry

    lax.fori_loop(1, GROUPS, dispatch_and_send, 0)

    drain(labels_in, plane_label_recv)
    row_rank = iota((SLOTS, 128), 0) & (CAP - 1)
    lane = iota((SLOTS, 128), 1)

    plane_step = iota((SLOTS, 128), 0) >> 6

    def codes(group):
        marks = labels_in[pl.ds(group * PLANE_GROUP, PLANE_GROUP)]
        spread = jnp.broadcast_to(marks.reshape(PER_GROUP, 1, 128), (PER_GROUP, CAP, 128)).reshape(SLOTS, 128)
        at = ((plane_step + group * PLANE_GROUP) & 15) * CAP + row_rank
        mark = jnp.sum(jnp.where(lane == at, spread, 0.0), axis=1, keepdims=True)
        return (mark.astype(jnp.int32) - 1) == iota((SLOTS, ROWS), 1)

    def count(group, used):
        return used + jnp.sum(jnp.where(codes(group), 1.0, 0.0), axis=0, keepdims=True)

    used = lax.fori_loop(0, GROUPS, count, jnp.zeros((1, ROWS), F32))
    used_out[...] = used
    wanted = jnp.where(used > 0.0, 8 * ROWS, source[...])
    wanted_here[...] = wanted
    for j in range(3):
        peer = {"narrow": lax.rem(narrow + j + 1, 4)}
        remote(wanted_here, asked.at[j], ask_send, ask_recv.at[j], peer).start()
    fetch_rank = fetch_ranks(wanted, before[...])
    far = ((wanted >> 10) != narrow) & (used == 0.0)
    over = jnp.max(jnp.where(far & (fetch_rank >= FETCH), 1.0, 0.0), axis=1, keepdims=True)
    results_out[:, DEPTH] = jnp.broadcast_to(over.reshape(1, 1, 1), (PLANE, 1, 128))

    for copy in loads[4:]:
        copy.wait()
    eff = nn(codebook[...], linear_map[...]).astype(BF16)
    effective[...] = eff
    eff_f = eff.astype(F32)
    norms = jnp.sum(eff_f * eff_f, axis=1, keepdims=True)
    code_norm[...] = jnp.transpose(jnp.broadcast_to(norms, (ROWS, 128)))[0:1, :]
    total[...] = jnp.zeros_like(total)

    for j in range(3):
        drain(asked.at[j], ask_recv.at[j])
        theirs = asked[j]
        order = fetch_ranks(theirs, before[...])
        mine = ((theirs >> 10) == narrow) & (order == iota((FETCH, ROWS), 0))
        index = jnp.sum(jnp.where(mine, (theirs & 1023).astype(F32), 0.0), axis=1, keepdims=True)
        rows = one(index.astype(jnp.int32) == iota((FETCH, ROWS), 1))
        rows_out[j] = nn(rows, frames[...]).astype(BF16)

    mine = ((wanted >> 10) == narrow) & ((wanted & 1023) == iota((ROWS, ROWS), 0))
    used_column = jnp.transpose(jnp.broadcast_to(used, (128, ROWS)))[:, 0:1]
    fresh[...] = jnp.where(used_column > 0.0, codebook[...].astype(F32), tn(one(mine), frames[...])).astype(BF16)
    asked_for = [
        jnp.where(((wanted >> 10) == lax.rem(narrow + j + 1, 4)) & (fetch_rank == iota((FETCH, ROWS), 0)), 1.0, 0.0)
        for j in range(3)
    ]
    spare = FETCHED - 3 * FETCH
    picks[...] = jnp.transpose(jnp.concatenate(asked_for + [jnp.zeros((spare, ROWS), F32)], axis=0)).astype(BF16)
    rows_in[pl.ds(3 * FETCH, spare), :] = jnp.zeros((spare, WIDTH), BF16)

    def work(group, carry):
        rows = pl.ds(pl.multiple_of(group * 2 * SLOTS, 2 * SLOTS), 2 * SLOTS)
        drain(arrived.at[rows], data_recv.at[group])

        @pl.when(group == SEND_AT)
        def _():
            for j in range(3):
                peer = {"narrow": lax.rem(narrow + 3 - j, 4)}
                remote(
                    rows_out.at[j], rows_in.at[pl.ds(j * FETCH, FETCH)], row_send, row_recv.at[j], peer
                ).start()

        parts = arrived[rows, :].astype(F32).reshape(PER_GROUP, 2, CAP, HALF)
        taken_f = jnp.concatenate(
            [parts[:, 0].reshape(SLOTS, HALF), parts[:, 1].reshape(SLOTS, HALF)], axis=1
        )
        taken = taken_f.astype(BF16)
        chosen_mask = codes(group)
        selector = one(chosen_mask)
        quantized = nn(selector, effective[...])
        chosen = nn(selector, codebook[...]).astype(BF16)
        gap = quantized - taken_f
        commitment = jnp.sum(gap * gap, axis=1, keepdims=True) * (1.0 / WIDTH)
        cross = nt(taken, effective[...])
        least = jnp.min(code_norm[...] - 2.0 * cross, axis=1, keepdims=True)
        nearest = (jnp.sum(taken_f * taken_f, axis=1, keepdims=True) + least) * (1.0 / WIDTH)
        total[...] += tn(chosen, gap.astype(BF16)).reshape(total.shape)
        at = ((plane_step + group * PLANE_GROUP) & 7) * (2 * CAP) + row_rank
        back = jnp.where(lane == at, commitment, 0.0) + jnp.where(lane == at + CAP, nearest, 0.0)
        back = jnp.sum(back.reshape(PER_GROUP, CAP, 128), axis=1, keepdims=True)
        results_out[pl.ds(group * PLANE_GROUP, PLANE_GROUP), pl.ds(0, DEPTH)] = back.reshape(PLANE_GROUP, DEPTH, 1, 128)

        def give(step):
            remote(
                results_out.at[step], results_mid.at[step], plane_result_send, plane_result_recv,
                target(plane_index(step, here, -1), 0),
            ).start()

        @pl.when(group > 0)
        def _():
            give(group * PLANE_GROUP)

        @pl.when(group == 0)
        def _():
            pltpu.make_async_copy(results_out.at[0], results_mid.at[0], plane_result_recv).start()

        for step in range(1, PLANE_GROUP):
            give(group * PLANE_GROUP + step)
        return carry

    lax.fori_loop(0, GROUPS, work, 0)

    to_pair = remote(total.at[:, :, :, 1 - core], half_in, half_send, half_recv, device(x, y, z, 1 - core))
    to_pair.start()

    to_pair.wait()
    half_sum[...] = total[:, :, :, core] + half_in[...]
    for step in range(1, 16):
        x2 = lax.rem(x + step % 4, 4)
        y2 = lax.rem(y + step // 4, 4)
        remote(
            half_sum.at[y2, :, x2], plane_in.at[step - 1], plane_send, plane_recv, device(x2, y2, z, core)
        ).start()

    drain(results_mid, plane_result_recv)
    for block in range(4):
        results_pack[:, block] = jnp.sum(results_mid[pl.ds(block * 8, 8), pl.ds(0, DEPTH)], axis=0)
    results_pack[:, 4] = jnp.broadcast_to(jnp.max(results_mid[:, DEPTH], axis=0, keepdims=True), (DEPTH, 1, 128))
    results_in[0] = results_pack[0]
    for step in range(1, DEPTH):
        offset_wide, narrow_back = column_index(step, here, -1)
        remote(
            results_pack.at[step], results_in.at[step], column_result_send, column_result_recv,
            {"wide": plane_here + offset_wide, "narrow": narrow_back},
        ).start()

    drain(plane_in, plane_recv)
    plane_sum[...] = half_sum[y, :, x] + jnp.sum(plane_in[...], axis=0)
    for step in range(1, 8):
        z2 = lax.rem(z + step, 8)
        remote(
            plane_sum.at[z2 // 4], column_in.at[step - 1], column_send, column_recv, device(x, y, z2, core)
        ).start()

    drain(results_in.at[pl.ds(1, DEPTH - 1)], column_result_recv)
    over_out[...] = jnp.max(results_in[:, 4], axis=0)
    returned = results_in[:, pl.ds(0, 4)].reshape(PLANE, 128)
    step_of = place[0:1, :]
    steps = one((step_of & 7) * 4 + (step_of >> 6) == iota((PLANE, ROWS), 0))
    first = returned.astype(BF16)
    rest = returned - first.astype(F32)
    second = rest.astype(BF16)
    third = (rest - second.astype(F32)).astype(BF16)
    home = tn(first, steps) + tn(second, steps) + tn(third, steps)
    at = ((step_of >> 3) & 7) * (2 * CAP) + place[1:2, :]
    commit_out[...] = jnp.sum(jnp.where(at == iota((128, ROWS), 0), home, 0.0), axis=0, keepdims=True)
    near_out[...] = jnp.sum(jnp.where(at + CAP == iota((128, ROWS), 0), home, 0.0), axis=0, keepdims=True)

    for j in range(3):
        drain(rows_in.at[pl.ds(j * FETCH, FETCH)], row_recv.at[j])
    fresh_out[...] = (fresh[...].astype(F32) + nn(picks[...], rows_in[...])).astype(BF16)

    drain(column_in, column_recv)
    grad_out[...] = (plane_sum[z // 4] + jnp.sum(column_in[...], axis=0)) * (2.0 / 512.0)

    sent = pl.ds(BLOCK, (DEVICES - 1) * BLOCK)
    drain(outgoing.at[sent], data_send)
    drain(labels_mid.at[pl.ds(1, DEPTH - 1)], column_label_send)
    drain(labels_in.at[pl.ds(1, PLANE - 1)], plane_label_send)
    drain(results_mid.at[pl.ds(1, PLANE - 1)], plane_result_send)
    drain(results_in.at[pl.ds(1, DEPTH - 1)], column_result_send)
    drain(plane_in, plane_send)
    drain(column_in, column_send)
    drain(asked, ask_send)
    drain(rows_out, row_send)


def exchange(frames, codebook, linear_map, tile, offset, source):
    vmem = pl.BlockSpec(memory_space=pltpu.VMEM)
    dma = pltpu.SemaphoreType.DMA
    return pl.pallas_call(
        step_kernel,
        out_shape=[
            jax.ShapeDtypeStruct((1, ROWS), F32),
            jax.ShapeDtypeStruct((1, ROWS), F32),
            jax.ShapeDtypeStruct((CAP, WIDTH), F32),
            jax.ShapeDtypeStruct((ROWS, WIDTH), BF16),
            jax.ShapeDtypeStruct((1, ROWS), F32),
            jax.ShapeDtypeStruct((1, 128), F32),
        ],
        in_specs=[pl.BlockSpec(memory_space=pl.ANY)] * 6,
        out_specs=[vmem] * 6,
        scratch_shapes=[
            pltpu.VMEM((ROWS, WIDTH), BF16),
            pltpu.VMEM((ROWS, WIDTH), BF16),
            pltpu.VMEM((WIDTH, WIDTH), BF16),
            pltpu.VMEM((1, ROWS), jnp.int32),
            pltpu.VMEM((1, ROWS), jnp.int32),
            pltpu.VMEM((1, ROWS), jnp.int32),
            pltpu.VMEM((1, ROWS), jnp.int32),
            pltpu.VMEM((DEVICES * BLOCK, HALF), BF16),
            pltpu.VMEM((DEVICES * BLOCK, HALF), BF16),
            pltpu.VMEM((DEPTH, 2, 1, 128), F32),
            pltpu.VMEM((DEPTH, 2, 1, 128), F32),
            pltpu.VMEM((PLANE, DEPTH, 1, 128), F32),
            pltpu.VMEM((PLANE, DEPTH + 1, 1, 128), F32),
            pltpu.VMEM((PLANE, DEPTH + 1, 1, 128), F32),
            pltpu.VMEM((DEPTH, 5, 1, 128), F32),
            pltpu.VMEM((DEPTH, 5, 1, 128), F32),
            pltpu.VMEM((ROWS, ROWS), BF16),
            pltpu.VMEM((ROWS, WIDTH), BF16),
            pltpu.VMEM((1, ROWS), F32),
            pltpu.VMEM((8, ROWS), jnp.int32),
            pltpu.VMEM((4, 2, 4, 2, 8, WIDTH), F32),
            pltpu.VMEM((4, 2, 4, 8, WIDTH), F32),
            pltpu.VMEM((4, 2, 4, 8, WIDTH), F32),
            pltpu.VMEM((15, 2, 8, WIDTH), F32),
            pltpu.VMEM((2, 8, WIDTH), F32),
            pltpu.VMEM((7, 8, WIDTH), F32),
            pltpu.VMEM((3, 1, ROWS), jnp.int32),
            pltpu.VMEM((3, FETCH, WIDTH), BF16),
            pltpu.VMEM((FETCHED, WIDTH), BF16),
            pltpu.VMEM((ROWS, FETCHED), BF16),
            pltpu.VMEM((ROWS, WIDTH), BF16),
            dma((6,)), dma, dma((GROUPS,)), dma, dma, dma, dma,
            dma, dma, dma, dma,
            dma, dma, dma, dma, dma, dma,
            dma, dma((3,)), dma, dma((3,)),
        ],
        compiler_params=pltpu.CompilerParams(
            collective_id=0, has_side_effects=True, vmem_limit_bytes=60 * 2**20
        ),
    )(frames, codebook, linear_map, tile, offset, source)


def shards(frames, codebook, linear_map, code_tile, code_offset, reinit_source):
    commitment, nearest, gradient, fresh, used, over = exchange(
        frames,
        codebook,
        linear_map,
        code_tile.reshape(1, ROWS),
        code_offset.reshape(1, ROWS),
        reinit_source.reshape(1, ROWS),
    )

    def whole_gather():
        here = lax.axis_index("narrow")
        owner = reinit_source >> 10
        row = reinit_source & (ROWS - 1)
        result = jnp.where((owner == here)[:, None], frames[row], codebook)
        for shift in range(1, 4):
            theirs = lax.ppermute(frames, "narrow", [(j, (j - shift) % 4) for j in range(4)])
            result = jnp.where((owner == lax.rem(here + shift, 4))[:, None], theirs[row], result)
        return jnp.where(used.reshape(ROWS, 1) > 0.0, codebook, result)

    new_codebook = lax.cond(over[0, 127] > 0.0, whole_gather, lambda: fresh)
    return commitment.reshape(ROWS), nearest.reshape(ROWS), gradient, new_codebook


def solution(mesh):
    placed = (
        P(("wide", "narrow"), None),
        P(("wide", "narrow"), None),
        P(),
        P(("wide", "narrow"), None),
        P(("wide", "narrow")),
        P(("wide", "narrow")),
    )
    return jax.shard_map(
        shards,
        mesh=mesh,
        in_specs=placed,
        out_specs=(
            P(("wide", "narrow")),
            P(("wide", "narrow")),
            P("wide", None),
            P(("wide", "narrow"), None),
        ),
        check_vma=False,
    )
```

time: 131 us -> 105 us (0.80); the launches traced: 129 us -> 104 us
  between operations: 14.7 us -> 1.35 us
  Pallas kernels: 109 us -> 97.8 us
    pallas_call x1, Pallas kernels: 109 us -> 97.8 us  [exchange(): pl.pallas_call(step_kernel, out_shape=[jax.ShapeDtypeStruct((1, ROWS), F3...]
    unnamed x10 -> x16, local copies, waits for them, and re-layouts: 5.17 us -> 4.69 us
where the time goes in v2:
time: 105 us; the launch traced here: 104 us
  Pallas kernels  97.8 us (93%)
  local copies, waits for them, and re-layouts  5.27 us (5%)
  between operations  1.35 us (1%)
    pallas_call x1, Pallas kernels, exchange(): pl.pallas_call(step_kernel, out_shape=[jax.ShapeDtypeStruct((1, ROWS), F3...  97.8 us
    unnamed x16, local copies, waits for them, and re-layouts  4.69 us

profile of v2, /device:TPU:8, one launch (start us, length us, event | category | flops | bytes accessed | tf_op | source)
XLA Modules:
  0.0 104.4 jit_solution(5254398856590962994)
XLA Ops:
  0.6 0.0 copy-start.3
  0.6 0.7 copy-done.3
  1.3 0.0 copy-start
  1.3 97.8 %shard_map.93 = (f32[1,1024]{1,0:T(1,128)}, f32[1,1024]{1,0:T(1,128)}, f32[8,512]{1,0:T(8,128)}, bf16[1024,512]{1,0:T(8,128)(2,1)S(1)}, f32[1,1024]{1,0:T(1,128)S(1)}, /*index=5*/f32[1,128]{1,0:T(1,128)}) custom-call(bf16[1024,512]{1,0:T(8,128)(2,1)} %frames_in.1, bf16[1024,512]{1,0:T(8,128)(2,1)} %codebook_in.1, bf16[512,512]{1,0:T(8,128)(2,1)} %linear_in.1, ...), custom_call_target="tpu_custom_call" | custom-call | tf_op jit(solution)/shard_map/pallas_call | solution.py:405
  99.1 0.0 copy-start.7
  99.1 0.6 copy-done.7
  99.7 0.6 slice.3
  101.0 0.0 copy-done
  101.0 0.0 copy-start.6
  101.0 0.0 copy-start.5
  101.0 0.0 copy-start.4
  101.0 0.6 copy-done.6
  101.6 0.6 copy.16
  102.2 0.0 copy-done.5
  102.2 0.6 copy.17
  102.8 0.0 copy-done.4
  102.8 0.6 copy.18
  103.4 1.0 copy.19
  (1 shorter events, 0.0 us)
Async XLA Ops:
  0.6 0.7 copy-start.3
  1.3 99.7 %copy-start = (bf16[1024,512]{1,0:T(8,128)(2,1)S(1)}, bf16[1024,512]{1,0:T(8,128)(2,1)}, u32[]{:S(2)}) copy-start(bf16[1024,512]{1,0:T(8,128)(2,1)} %frames_in.1) | copy-start | bytes 3145732
  99.1 0.6 copy-start.7
  101.0 0.7 copy-start.6
  101.0 1.3 %copy-start.5 = (f32[1,1024]{1,0:T(1,128)S(1)}, f32[1,1024]{1,0:T(1,128)}, u32[]{:S(2)}) copy-start(f32[1,1024]{1,0:T(1,128)} %get-tuple-element.27) | copy-start | bytes 12292
  101.0 1.8 %copy-start.4 = (f32[8,512]{1,0:T(8,128)S(1)}, f32[8,512]{1,0:T(8,128)}, u32[]{:S(2)}) copy-start(f32[8,512]{1,0:T(8,128)} %get-tuple-element.42) | copy-start | bytes 49156

commit v3 on v2

--- a/solution.py
+++ b/solution.py
@@ -22,6 +22,7 @@
 BLOCK = 2 * CAP
 FETCH = 208
 SEND_AT = 7
+EARLY = 2
 PLANE = 32
 DEPTH = 8
 PLANE_GROUP = PLANE // GROUPS
@@ -223,7 +224,7 @@
         lax.fori_loop(group * PLANE_GROUP, (group + 1) * PLANE_GROUP, send_plane, 0)
         return carry
 
-    lax.fori_loop(1, GROUPS, dispatch_and_send, 0)
+    lax.fori_loop(1, EARLY, dispatch_and_send, 0)
 
     drain(labels_in, plane_label_recv)
     row_rank = iota((SLOTS, 128), 0) & (CAP - 1)
@@ -248,6 +249,7 @@
     for j in range(3):
         peer = {"narrow": lax.rem(narrow + j + 1, 4)}
         remote(wanted_here, asked.at[j], ask_send, ask_recv.at[j], peer).start()
+    lax.fori_loop(EARLY, GROUPS, dispatch_and_send, 0)
     fetch_rank = fetch_ranks(wanted, before[...])
     far = ((wanted >> 10) != narrow) & (used == 0.0)
     over = jnp.max(jnp.where(far & (fetch_rank >= FETCH), 1.0, 0.0), axis=1, keepdims=True)
@@ -367,7 +369,7 @@
         ).start()
 
     drain(results_in.at[pl.ds(1, DEPTH - 1)], column_result_recv)
-    over_out[...] = jnp.max(results_in[:, 4], axis=0)
+    over_out[0, 0] = jnp.max(results_in[:, 4]).astype(jnp.int32)
     returned = results_in[:, pl.ds(0, 4)].reshape(PLANE, 128)
     step_of = place[0:1, :]
     steps = one((step_of & 7) * 4 + (step_of >> 6) == iota((PLANE, ROWS), 0))
@@ -410,10 +412,10 @@
             jax.ShapeDtypeStruct((CAP, WIDTH), F32),
             jax.ShapeDtypeStruct((ROWS, WIDTH), BF16),
             jax.ShapeDtypeStruct((1, ROWS), F32),
-            jax.ShapeDtypeStruct((1, 128), F32),
+            jax.ShapeDtypeStruct((1, 1), jnp.int32),
         ],
         in_specs=[pl.BlockSpec(memory_space=pl.ANY)] * 6,
-        out_specs=[vmem] * 6,
+        out_specs=[vmem] * 5 + [pl.BlockSpec(memory_space=pltpu.SMEM)],
         scratch_shapes=[
             pltpu.VMEM((ROWS, WIDTH), BF16),
             pltpu.VMEM((ROWS, WIDTH), BF16),
@@ -457,6 +459,26 @@
     )(frames, codebook, linear_map, tile, offset, source)
 
 
+def publish_kernel(*refs):
+    sources, results, sems = refs[:4], refs[4:8], refs[8]
+    copies = [pltpu.make_async_copy(src, dst, sems.at[i]) for i, (src, dst) in enumerate(zip(sources, results))]
+    for copy in copies:
+        copy.start()
+    for copy in copies:
+        copy.wait()
+
+
+def publish(*arrays):
+    anywhere = pl.BlockSpec(memory_space=pl.ANY)
+    return pl.pallas_call(
+        publish_kernel,
+        out_shape=[jax.ShapeDtypeStruct(a.shape, a.dtype) for a in arrays],
+        in_specs=[anywhere] * 4,
+        out_specs=[anywhere] * 4,
+        scratch_shapes=[pltpu.SemaphoreType.DMA((4,))],
+    )(*arrays)
+
+
 def shards(frames, codebook, linear_map, code_tile, code_offset, reinit_source):
     commitment, nearest, gradient, fresh, used, over = exchange(
         frames,
@@ -477,7 +499,8 @@
             result = jnp.where((owner == lax.rem(here + shift, 4))[:, None], theirs[row], result)
         return jnp.where(used.reshape(ROWS, 1) > 0.0, codebook, result)
 
-    new_codebook = lax.cond(over[0, 127] > 0.0, whole_gather, lambda: fresh)
+    new_codebook = lax.cond(over[0, 0] > 0, whole_gather, lambda: fresh)
+    commitment, nearest, gradient, new_codebook = publish(commitment, nearest, gradient, new_codebook)
     return commitment.reshape(ROWS), nearest.reshape(ROWS), gradient, new_codebook
 
 

time: 105 us -> 93.9 us (0.89)
  Pallas kernels: 97.8 us -> 90.6 us
  local copies, waits for them, and re-layouts: 5.27 us -> 0.68 us
    pallas_call x1, Pallas kernels: 97.8 us -> 88.7 us  [exchange(): pl.pallas_call(step_kernel, out_shape=[jax.ShapeDtypeStruct((1, ROWS), F3...]
    unnamed x16 -> x4, local copies, waits for them, and re-layouts: 4.69 us -> 0.68 us
    pallas_call x0 -> x1, Pallas kernels: none -> 1.89 us  [publish(): pl.pallas_call(publish_kernel, out_shape=[jax.ShapeDtypeStruct(a.shape, a...]
where the time goes in v3:
time: 93.9 us; the launch traced here: 92.6 us
  Pallas kernels  90.6 us (96%)
  between operations  1.29 us (1%)
    pallas_call x1, Pallas kernels, exchange(): pl.pallas_call(step_kernel, out_shape=[jax.ShapeDtypeStruct((1, ROWS), F3...  88.7 us
    pallas_call x1, Pallas kernels, publish(): pl.pallas_call(publish_kernel, out_shape=[jax.ShapeDtypeStruct(a.shape, a...  1.89 us

profile of v3, /device:TPU:8, one launch (start us, length us, event | category | flops | bytes accessed | tf_op | source)
XLA Modules:
  0.0 92.6 jit_solution(10773483942416440875)
XLA Ops:
  0.6 0.0 copy-start.3
  0.6 0.7 copy-done.3
  1.3 0.0 copy-start
  1.3 88.7 %shard_map.93 = (f32[1,1024]{1,0:T(1,128)}, f32[1,1024]{1,0:T(1,128)}, f32[8,512]{1,0:T(8,128)}, bf16[1024,512]{1,0:T(8,128)(2,1)S(1)}, f32[1,1024]{1,0:T(1,128)S(1)}, /*index=5*/s32[1,1]{1,0:T(1,128)}) custom-call(bf16[1024,512]{1,0:T(8,128)(2,1)} %frames_in.1, bf16[1024,512]{1,0:T(8,128)(2,1)} %codebook_in.1, bf16[512,512]{1,0:T(8,128)(2,1)} %linear_in.1, ...), custom_call_target="tpu_custom_call" | custom-call | tf_op jit(solution)/shard_map/pallas_call | solution.py:407
  90.7 0.0 copy-done
  90.7 1.9 %shard_map.94 = (f32[1,1024]{1,0:T(1,128)}, f32[1,1024]{1,0:T(1,128)}, f32[8,512]{1,0:T(8,128)}, bf16[1024,512]{1,0:T(8,128)(2,1)}) custom-call(f32[1,1024]{1,0:T(1,128)} %get-tuple-element.30.refs_0_, f32[1,1024]{1,0:T(1,128)} %get-tuple-element.31.refs_1_, f32[8,512]{1,0:T(8,128)} %get-tuple-element.32.refs_2_, bf16[1024,512]{1,0:T(8,128)(2,1)S(1)} %get-tuple-element.44.refs_3_), custom_call_target="tpu_custom_call" | custom-call | tf_op jit(solution)/shard_map/pallas_call | solution.py:473
  (1 shorter events, 0.0 us)
Async XLA Ops:
  0.6 0.7 copy-start.3
  1.3 89.4 %copy-start = (bf16[1024,512]{1,0:T(8,128)(2,1)S(1)}, bf16[1024,512]{1,0:T(8,128)(2,1)}, u32[]{:S(2)}) copy-start(bf16[1024,512]{1,0:T(8,128)(2,1)} %frames_in.1) | copy-start | bytes 3145732

commit v4 on v3

--- a/solution.py
+++ b/solution.py
@@ -20,8 +20,8 @@
 SLOTS = PER_GROUP * CAP
 HALF = WIDTH // 2
 BLOCK = 2 * CAP
-FETCH = 208
-SEND_AT = 7
+FETCH = 192
+SEND_AT = (6, 6, 8)
 EARLY = 2
 PLANE = 32
 DEPTH = 8
@@ -167,7 +167,6 @@
     labels_out[:, 0] = marks[:, :128].reshape(DEPTH, 1, 128)
     labels_out[:, 1] = marks[:, 128:].reshape(DEPTH, 1, 128)
     labels_mid[0] = labels_out[0]
-    loads[3].wait()
 
     def dispatch(group):
         slots = iota((SLOTS, ROWS), 0) + group * SLOTS
@@ -177,8 +176,6 @@
         block = jnp.concatenate([left, right], axis=1).reshape(2 * SLOTS, HALF)
         outgoing[pl.ds(pl.multiple_of(group * 2 * SLOTS, 2 * SLOTS), 2 * SLOTS), :] = block.astype(BF16)
 
-    dispatch(0)
-
     pl.semaphore_wait(barrier, DEPTH + PLANE - 2)
 
     for step in range(1, DEPTH):
@@ -186,6 +183,8 @@
             labels_out.at[step], labels_mid.at[step], column_label_send, column_label_recv,
             target(plane_here, step),
         ).start()
+    loads[3].wait()
+    dispatch(0)
     drain(labels_mid.at[pl.ds(1, DEPTH - 1)], column_label_recv)
 
     own_label = pltpu.make_async_copy(labels_mid.at[:, 0], labels_in.at[0], plane_label_recv)
@@ -284,17 +283,19 @@
     picks[...] = jnp.transpose(jnp.concatenate(asked_for + [jnp.zeros((spare, ROWS), F32)], axis=0)).astype(BF16)
     rows_in[pl.ds(3 * FETCH, spare), :] = jnp.zeros((spare, WIDTH), BF16)
 
+    def respond(j):
+        peer = {"narrow": lax.rem(narrow + 3 - j, 4)}
+        remote(
+            rows_out.at[j], rows_in.at[pl.ds(j * FETCH, FETCH)], row_send, row_recv.at[j], peer
+        ).start()
+
     def work(group, carry):
         rows = pl.ds(pl.multiple_of(group * 2 * SLOTS, 2 * SLOTS), 2 * SLOTS)
         drain(arrived.at[rows], data_recv.at[group])
 
-        @pl.when(group == SEND_AT)
-        def _():
-            for j in range(3):
-                peer = {"narrow": lax.rem(narrow + 3 - j, 4)}
-                remote(
-                    rows_out.at[j], rows_in.at[pl.ds(j * FETCH, FETCH)], row_send, row_recv.at[j], peer
-                ).start()
+        for j in range(3):
+            if SEND_AT[j] < GROUPS:
+                pl.when(group == SEND_AT[j])(functools.partial(respond, j))
 
         parts = arrived[rows, :].astype(F32).reshape(PER_GROUP, 2, CAP, HALF)
         taken_f = jnp.concatenate(
@@ -359,6 +360,9 @@
             results_pack.at[step], results_in.at[step], column_result_send, column_result_recv,
             {"wide": plane_here + offset_wide, "narrow": narrow_back},
         ).start()
+    for j in range(3):
+        if SEND_AT[j] == GROUPS:
+            respond(j)
 
     drain(plane_in, plane_recv)
     plane_sum[...] = half_sum[y, :, x] + jnp.sum(plane_in[...], axis=0)

time: 93.9 us -> 88.9 us (0.947)
  Pallas kernels: 90.6 us -> 85.3 us
    pallas_call x1, Pallas kernels: 88.7 us -> 83.4 us  [exchange(): pl.pallas_call(step_kernel, out_shape=[jax.ShapeDtypeStruct((1, ROWS), F3...]
where the time goes in v4:
time: 88.9 us; the launch traced here: 87.3 us
  Pallas kernels  85.3 us (96%)
  between operations  1.29 us (1%)
    pallas_call x1, Pallas kernels, exchange(): pl.pallas_call(step_kernel, out_shape=[jax.ShapeDtypeStruct((1, ROWS), F3...  83.4 us
    pallas_call x1, Pallas kernels, publish(): pl.pallas_call(publish_kernel, out_shape=[jax.ShapeDtypeStruct(a.shape, a...  1.89 us

profile of v4, /device:TPU:8, one launch (start us, length us, event | category | flops | bytes accessed | tf_op | source)
XLA Modules:
  0.0 87.3 jit_solution(7249470500043977915)
XLA Ops:
  0.6 0.0 copy-start.3
  0.6 0.7 copy-done.3
  1.3 0.0 copy-start
  1.3 83.4 %shard_map.93 = (f32[1,1024]{1,0:T(1,128)}, f32[1,1024]{1,0:T(1,128)}, f32[8,512]{1,0:T(8,128)}, bf16[1024,512]{1,0:T(8,128)(2,1)S(1)}, f32[1,1024]{1,0:T(1,128)S(1)}, /*index=5*/s32[1,1]{1,0:T(1,128)}) custom-call(bf16[1024,512]{1,0:T(8,128)(2,1)} %frames_in.1, bf16[1024,512]{1,0:T(8,128)(2,1)} %codebook_in.1, bf16[512,512]{1,0:T(8,128)(2,1)} %linear_in.1, ...), custom_call_target="tpu_custom_call" | custom-call | tf_op jit(solution)/shard_map/pallas_call | solution.py:411
  85.4 0.0 copy-done
  85.4 1.9 %shard_map.94 = (f32[1,1024]{1,0:T(1,128)}, f32[1,1024]{1,0:T(1,128)}, f32[8,512]{1,0:T(8,128)}, bf16[1024,512]{1,0:T(8,128)(2,1)}) custom-call(f32[1,1024]{1,0:T(1,128)} %get-tuple-element.30.refs_0_, f32[1,1024]{1,0:T(1,128)} %get-tuple-element.31.refs_1_, f32[8,512]{1,0:T(8,128)} %get-tuple-element.32.refs_2_, bf16[1024,512]{1,0:T(8,128)(2,1)S(1)} %get-tuple-element.44.refs_3_), custom_call_target="tpu_custom_call" | custom-call | tf_op jit(solution)/shard_map/pallas_call | solution.py:477
  (1 shorter events, 0.0 us)
Async XLA Ops:
  0.6 0.7 copy-start.3
  1.3 84.0 %copy-start = (bf16[1024,512]{1,0:T(8,128)(2,1)S(1)}, bf16[1024,512]{1,0:T(8,128)(2,1)}, u32[]{:S(2)}) copy-start(bf16[1024,512]{1,0:T(8,128)(2,1)} %frames_in.1) | copy-start | bytes 3145732
